TPU v7x, 256 devices: a whole 4x4x8 slice. The times are simulated.
256 devices in a mesh: lat: 8 (over y_hi, x), lon: 32 (over y_lo, z, core).
Axes of the slice: x: 4, y: 4 (y_hi: 2, y_lo: 2; y = y_hi * 2 + y_lo), z: 8, core: 2. Of those that a mesh axis runs over, the one named last changes fastest.
Arguments:
- state: bfloat16 [128, 128, 4096], P(None, 'lat', 'lon'), may hold values from -6 to 6
- heat_cot: bfloat16 [128, 128, 4096], P(None, 'lat', 'lon'), may hold values from -6 to 6
- state_cot: float32 [128, 128, 4096], P(None, 'lat', 'lon'), may hold values from -6 to 6
- courant_lon: bfloat16 [128, 128, 4096], P(None, 'lat', 'lon'), may hold values from -0.29882812 to 0.29882812
- courant_lat: bfloat16 [128, 128, 4096], P(None, 'lat', 'lon'), may hold values from -0.29882812 to 0.29882812
- w_first: bfloat16 [512, 128], replicated, may hold values from -0.5 to 0.5
- w_second: bfloat16 [512, 512], replicated, may hold values from -0.25 to 0.25
- w_third: bfloat16 [128, 512], replicated, may hold values from -0.25 to 0.25
Outputs:
- state_grad: float32 [128, 128, 4096], P(None, 'lat', 'lon')
- grad_first: float32 [512, 128], replicated
- grad_second: float32 [512, 512], replicated
- grad_third: float32 [128, 512], replicated
All inputs are finite; a program needn't handle non-finite values.
Results may differ from a plain program's by a relative error of at most 0.006.
Values may be sent and summed in bfloat16 or wider, within the bound.
A program may use at most 128 MiB of HBM per device.

v0:
```python
import math

import jax
import jax.numpy as jnp
from jax import lax
from jax.sharding import PartitionSpec as P

SUBSTEPS = 3


EPSILON = 1e-05


def from_behind(block, axis, distance):
    devices = range(lax.axis_size(axis))
    route = [(i - distance, i) for i in devices if i - distance in devices]
    return lax.ppermute(block, axis, route)


def shifted(x, axis, by):
    count = lax.axis_size(axis)
    return lax.ppermute(x, axis, [(i, (i + by) % count) for i in range(count)])


def padded_2(cells, sides, width, closed):
    for axis, dim in sides:
        count = lax.axis_size(axis)
        ends = count if closed else count - 1
        head = lax.slice_in_dim(cells, 0, width, axis=dim)
        tail = lax.slice_in_dim(cells, cells.shape[dim] - width, cells.shape[dim], axis=dim)
        cells = jnp.concatenate(
            [
                lax.ppermute(tail, axis, [(i, (i + 1) % count) for i in range(ends)]),
                cells,
                lax.ppermute(head, axis, [((i + 1) % count, i) for i in range(ends)]),
            ],
            axis=dim,
        )
    return cells


def silu_slope(pre):
    sigma = jax.nn.sigmoid(pre)
    return sigma * (1.0 + pre * (1.0 - sigma))


def contract_first(left, right):
    return lax.dot_general(
        left, right, (((0,), (0,)), ((), ())), preferred_element_type=jnp.float32
    )


def contract_last(left, right):
    return lax.dot_general(
        left, right, (((1,), (1,)), ((), ())), preferred_element_type=jnp.float32
    )


def adjoint_step(padded, lon_faces, lat_faces):
    centre = padded[:, 1:-1, 1:-1]
    rows_mid = padded[:, 1:-1, :]
    lon_diff = rows_mid[:, :, 1:] - rows_mid[:, :, :-1]
    east_term = jnp.maximum(lon_faces[:, 1:-1, 1:-1], 0.0) * lon_diff[:, :, 1:]
    west_term = jnp.minimum(lon_faces[:, 1:-1, :-2], 0.0) * lon_diff[:, :, :-1]
    cols_mid = padded[:, :, 1:-1]
    lat_diff = cols_mid[:, 1:, :] - cols_mid[:, :-1, :]
    north_term = jnp.maximum(lat_faces[:, 1:-1, 1:-1], 0.0) * lat_diff[:, 1:, :]
    south_term = jnp.minimum(lat_faces[:, :-2, 1:-1], 0.0) * lat_diff[:, :-1, :]
    return centre + east_term + west_term + north_term + south_term


def zero_layer(faces, axis_dim):
    shape = list(faces.shape)
    shape[axis_dim] = 1
    return jnp.zeros(tuple(shape), faces.dtype)


def local(state, heat_cot, state_cot, courant_lon, courant_lat, w_first, w_second, w_third):
    levels, lat_rows, lon_cols = state.shape
    column_count = lat_rows * lon_cols
    grad_scale = 1.0 / math.sqrt(column_count * lax.axis_size("lat") * lax.axis_size("lon"))
    values = state.reshape(levels, column_count).astype(jnp.float32)
    column_cot = heat_cot.reshape(levels, column_count)
    inverse = lax.rsqrt(jnp.mean(values * values, axis=0, keepdims=True) + EPSILON)
    normed = values * inverse
    inputs = normed.astype(jnp.bfloat16)
    pre_first = jnp.dot(w_first, inputs, preferred_element_type=jnp.float32)
    act_first = jax.nn.silu(pre_first).astype(jnp.bfloat16)
    pre_second = jnp.dot(w_second, act_first, preferred_element_type=jnp.float32)
    act_second = jax.nn.silu(pre_second).astype(jnp.bfloat16)
    term_third = contract_last(column_cot, act_second)
    back_second = (contract_first(w_third, column_cot) * silu_slope(pre_second)).astype(
        jnp.bfloat16
    )
    term_second = contract_last(back_second, act_first)
    back_first = (contract_first(w_second, back_second) * silu_slope(pre_first)).astype(
        jnp.bfloat16
    )
    term_first = contract_last(back_first, inputs)
    sum_first, sum_second, sum_third = lax.psum(
        (term_first, term_second, term_third), ("lat", "lon")
    )
    input_cot = contract_first(w_first, back_first)
    state_part = inverse * (
        input_cot - normed * jnp.mean(input_cot * normed, axis=0, keepdims=True)
    )
    cotangent = state_cot + state_part.reshape(levels, lat_rows, lon_cols)
    rim_width = 1
    wind_faces = jnp.stack([courant_lon, courant_lat])
    south_rows = from_behind(wind_faces[:, :, lat_rows - rim_width :, :], "lat", 1)
    north_rows = zero_layer(wind_faces, 2)
    wind_faces = jnp.concatenate([south_rows, wind_faces, north_rows], axis=2)
    west_cols = shifted(wind_faces[:, :, :, lon_cols - rim_width :], "lon", 1)
    east_cols = zero_layer(wind_faces, 3)
    wind_faces = jnp.concatenate([west_cols, wind_faces, east_cols], axis=3)
    wind_faces = wind_faces.astype(jnp.float32)
    for substep in range(SUBSTEPS):
        extended = padded_2(cotangent, (("lat", 1),), 1, False)
        extended = padded_2(extended, (("lon", 2),), 1, True)
        cotangent = adjoint_step(extended, wind_faces[0], wind_faces[1])
    return (cotangent, sum_first * grad_scale, sum_second * grad_scale, sum_third * grad_scale)


def solution(mesh):
    in_specs = (
        P(None, "lat", "lon"),
        P(None, "lat", "lon"),
        P(None, "lat", "lon"),
        P(None, "lat", "lon"),
        P(None, "lat", "lon"),
        P(),
        P(),
        P(),
    )
    out_specs = (P(None, "lat", "lon"), P(), P(), P())
    return jax.shard_map(local, mesh=mesh, in_specs=in_specs, out_specs=out_specs, check_vma=False)
```

profile of v0, /device:TPU:8, one launch (start us, length us, event | category | flops | bytes accessed | tf_op | source)
XLA Modules:
  0.0 392.2 jit_solution(17519183942868527573)
XLA Ops:
  8.5 3.5 collective-permute-start
  19.7 2.3 fusion
  28.1 3.4 collective-permute-start.2
  31.5 1.9 collective-permute-start.3
  33.4 4.1 %fusion.20 = f32[128,512]{0,1:T(8,128)} fusion(f32[2048,512]{0,1:T(8,128)} %copy-done.20, bf16[16,8,16,128]{3,2,1,0:T(8,128)(2,1)S(1)} %bitcast.102), kind=kOutput, calls=%fused_computation.57 | convolution fusion | flops 273678336 | bytes 4980736 | tf_op jit(solution)/shard_map/dot_general | solution.py:54
  39.1 2.4 copy.81
  43.4 2.5 copy.83
  46.4 2.1 collective-permute-start.5
  48.5 2.9 collective-permute-start.4
  52.7 2.5 copy.82
  55.2 3.4 maximum_convert_fusion
  58.6 2.1 slice_bitcast_fusion
  60.7 2.4 copy.84
  63.1 2.4 copy.86
  65.5 3.5 fusion.17
  71.3 4.3 %collective-permute-start.6 = (f32[128,1,128]{2,1,0:T(1,128)S(1)}, f32[128,1,128]{2,1,0:T(1,128)S(1)}, u32[]{:S(2)}, u32[]{:S(2)}) collective-permute-start(f32[128,1,128]{2,1,0:T(1,128)S(1)} %get-tuple-element.33), channel_id=1, source_target_pairs={{0,32},{32,64},{64,96},{96,128},{128,160},{160,192},{192,224},{1,3... | collective-permute-start | bytes 196616 | tf_op jit(solution)/shard_map/ppermute | solution.py:33
  76.9 2.2 fusion.48
  79.1 3.2 collective-permute-done.7
  82.5 2.1 fusion.42
  84.6 1.9 copy.87
  86.5 1.9 copy.89
  88.5 4.0 %collective-permute-start.8 = (f32[128,18,1]{0,1,2:T(8,128)S(1)}, f32[128,18,1]{0,1,2:T(8,128)S(1)}, u32[]{:S(2)}, u32[]{:S(2)}) collective-permute-start(f32[128,18,1]{0,1,2:T(8,128)S(1)} %copy.87), channel_id=1, source_target_pairs={{1,0},{2,1},{3,2},{4,3},{5,4},{6,5},{7,6},{8,7},{9,8},{10,9},{11,1... | collective-permute-start | bytes 27656 | tf_op jit(solution)/shard_map/ppermute | solution.py:35
  92.5 2.9 maximum_subtract_fusion.1
  98.8 3.5 fusion.16
  105.5 3.9 collective-permute-start.10
  112.4 5.6 %collective-permute-done.11 = f32[128,1,128]{2,1,0:T(1,128)S(1)} collective-permute-done((f32[128,1,128]{2,1,0:T(1,128)S(1)}, f32[128,1,128]{2,1,0:T(1,128)S(1)}, u32[]{:S(2)}, u32[]{:S(2)}) %collective-permute-start.11) | collective-permute-done | bytes 65568 | tf_op jit(solution)/shard_map/ppermute | solution.py:35
  119.9 1.9 copy.91
  122.4 3.8 collective-permute-start.12
  131.1 2.9 fusion.15
  134.9 2.3 fusion.23
  137.2 243.2 %all-reduce.3.cloned.1.call-done = (f32[512,128]{1,0:T(8,128)}, f32[512,512]{1,0:T(8,128)}, f32[128,512]{0,1:T(8,128)}) async-done(((f32[512,128]{1,0:T(8,128)}, f32[512,512]{1,0:T(8,128)}, f32[128,512]{0,1:T(8,128)}), (f32[512,128]{1,0:T(8,128)}, f32[512,512]{1,0:T(8,128)}, f32[128,512]{0,1:T(8,128)})) %all-reduce.3.cloned.1.call-update) | async-done | bytes 1572880 | tf_op jit(solution)/shard_map/psum | solution.py:100
  380.4 1.8 broadcast_multiply_fusion.2
  (121 shorter events, 44.5 us)
Async XLA Ops:
  7.2 9.2 %copy-start = (bf16[512,512]{1,0:T(8,128)(2,1)S(1)}, bf16[512,512]{1,0:T(8,128)(2,1)}, u32[]{:S(2)}) copy-start(bf16[512,512]{1,0:T(8,128)(2,1)} %param.14) | copy-start | bytes 1572868
  7.2 373.2 %all-reduce.3.cloned.1.call-start = ((), (), s32[]{:S(2)}) async-start(), calls=%async_computation | async-start | bytes 3145728 | tf_op jit(solution)/shard_map/psum | solution.py:100
  8.4 6.6 %copy-start.26 = (bf16[512,128]{1,0:T(8,128)(2,1)S(1)}, bf16[512,128]{1,0:T(8,128)(2,1)}, u32[]{:S(2)}) copy-start(bf16[512,128]{1,0:T(8,128)(2,1)} %param.13) | copy-start | bytes 393220
  8.5 29.2 %collective-permute-start = (bf16[2,128,1,128]{3,2,1,0:T(2,128)(2,1)S(1)}, bf16[2,128,1,128]{3,2,1,0:T(2,128)(2,1)S(1)}, u32[]{:S(2)}, u32[]{:S(2)}) collective-permute-start(bf16[2,128,1,128]{3,2,1,0:T(2,128)(2,1)S(1)} %pad_maximum_fusion.24), channel_id=1, source_target_pairs={{0,32},{32,64},{64,96},{96,128},{128,160},{160,192},{192,224},{1,3... | collective-permute-start | bytes 196616 | tf_op jit(solution)/shard_map/ppermute | solution.py:17
  25.5 7.9 %copy-start.28 = (bf16[128,16,128]{2,1,0:T(8,128)(2,1)S(1)}, bf16[128,16,128]{2,1,0:T(8,128)(2,1)}, u32[]{:S(2)}) copy-start(bf16[128,16,128]{2,1,0:T(8,128)(2,1)} %param.9) | copy-start | bytes 1572868
  27.2 24.1 %copy-start.7 = (f32[128,16,128]{2,1,0:T(8,128)}, f32[128,16,128]{2,1,0:T(8,128)S(1)}, u32[]{:S(2)}) copy-start(f32[128,16,128]{2,1,0:T(8,128)S(1)} %add.78) | copy-start | bytes 3145732
  28.1 13.4 %collective-permute-start.2 = (f32[128,1,128]{2,1,0:T(1,128)}, f32[128,1,128]{2,1,0:T(1,128)S(1)}, u32[]{:S(2)}, u32[]{:S(2)}) collective-permute-start(f32[128,1,128]{2,1,0:T(1,128)} %get-tuple-element.35), channel_id=1, source_target_pairs={{0,32},{32,64},{64,96},{96,128},{128,160},{160,192},{192,224},{1,3... | collective-permute-start | bytes 196616 | tf_op jit(solution)/shard_map/ppermute | solution.py:33
  31.5 6.2 %copy-start.17 = (bf16[128,16,128]{2,1,0:T(8,128)(2,1)S(1)}, bf16[128,16,128]{2,1,0:T(8,128)(2,1)}, u32[]{:S(2)}) copy-start(bf16[128,16,128]{2,1,0:T(8,128)(2,1)} %param.12) | copy-start | bytes 1572868
  31.5 6.2 %copy-start.18 = (bf16[128,16,128]{2,1,0:T(8,128)(2,1)S(1)}, bf16[128,16,128]{2,1,0:T(8,128)(2,1)}, u32[]{:S(2)}) copy-start(bf16[128,16,128]{2,1,0:T(8,128)(2,1)} %param.11) | copy-start | bytes 1572868
  31.5 10.0 %collective-permute-start.3 = (f32[128,1,128]{2,1,0:T(1,128)}, f32[128,1,128]{2,1,0:T(1,128)S(1)}, u32[]{:S(2)}, u32[]{:S(2)}) collective-permute-start(f32[128,1,128]{2,1,0:T(1,128)} %get-tuple-element.36), channel_id=1, source_target_pairs={{32,0},{64,32},{96,64},{128,96},{160,128},{192,160},{224,192},{33,... | collective-permute-start | bytes 196616 | tf_op jit(solution)/shard_map/ppermute | solution.py:35
  41.5 11.2 %collective-permute-start.1 = (bf16[2,128,18,1]{1,0,3,2:T(2,128)(2,1)}, bf16[2,128,18,1]{1,0,3,2:T(2,128)(2,1)}, u32[]{:S(2)}, u32[]{:S(2)}) collective-permute-start(bf16[2,128,18,1]{1,0,3,2:T(2,128)(2,1)} %copy.81), channel_id=1, source_target_pairs={{0,1},{1,2},{2,3},{3,4},{4,5},{5,6},{6,7},{7,8},{8,9},{9,10},{10,1... | collective-permute-start | bytes 27656 | tf_op jit(solution)/shard_map/ppermute | solution.py:22
  46.4 8.8 %copy-start.19 = (bf16[128,16,128]{2,1,0:T(8,128)(2,1)S(1)}, bf16[128,16,128]{2,1,0:T(8,128)(2,1)}, u32[]{:S(2)}) copy-start(bf16[128,16,128]{2,1,0:T(8,128)(2,1)} %param.11) | copy-start | bytes 1572868
  46.4 16.7 %collective-permute-start.5 = (f32[128,18,1]{0,1,2:T(8,128)S(1)}, f32[128,18,1]{0,1,2:T(8,128)}, u32[]{:S(2)}, u32[]{:S(2)}) collective-permute-start(f32[128,18,1]{0,1,2:T(8,128)S(1)} %copy.85), channel_id=1, source_target_pairs={{0,1},{1,2},{2,3},{3,4},{4,5},{5,6},{6,7},{7,8},{8,9},{9,10},{10,1... | collective-permute-start | bytes 27656 | tf_op jit(solution)/shard_map/ppermute | solution.py:33
  48.5 12.2 %collective-permute-start.4 = (f32[128,18,1]{0,1,2:T(8,128)}, f32[128,18,1]{0,1,2:T(8,128)}, u32[]{:S(2)}, u32[]{:S(2)}) collective-permute-start(f32[128,18,1]{0,1,2:T(8,128)} %copy.83), channel_id=1, source_target_pairs={{1,0},{2,1},{3,2},{4,3},{5,4},{6,5},{7,6},{8,7},{9,8},{10,9},{11,1... | collective-permute-start | bytes 27656 | tf_op jit(solution)/shard_map/ppermute | solution.py:35
  60.7 41.7 %copy-start.2 = (f32[128,18,130]{2,1,0:T(8,128)}, f32[128,18,130]{2,1,0:T(8,128)S(1)}, u32[]{:S(2)}) copy-start(f32[128,18,130]{2,1,0:T(8,128)S(1)} %get-tuple-element.23) | copy-start | bytes 3594244
  65.5 4.2 %copy-start.13 = (f32[128,17,128]{2,1,0:T(8,128)S(1)}, f32[128,17,128]{2,1,0:T(8,128)}, u32[]{:S(2)}) copy-start(f32[128,17,128]{2,1,0:T(8,128)} %maximum_subtract_fusion) | copy-start | bytes 3342340
  69.7 7.1 %copy-start.22 = (bf16[512,2048]{1,0:T(8,128)(2,1)S(1)}, bf16[512,2048]{1,0:T(8,128)(2,1)}, u32[]{:S(2)}) copy-start(bf16[512,2048]{1,0:T(8,128)(2,1)} %copy-done.21) | copy-start | bytes 6291460
  69.7 7.1 %copy-start.31 = (bf16[512,2048]{1,0:T(8,128)(2,1)S(1)}, bf16[512,2048]{1,0:T(8,128)(2,1)}, u32[]{:S(2)}) copy-start(bf16[512,2048]{1,0:T(8,128)(2,1)} %copy-done.30) | copy-start | bytes 6291460
  71.1 11.4 %copy-start.11 = (f32[128,16,128]{2,1,0:T(8,128)}, f32[128,16,128]{2,1,0:T(8,128)S(1)}, u32[]{:S(2)}) copy-start(f32[128,16,128]{2,1,0:T(8,128)S(1)} %fusion.31) | copy-start | bytes 3145732
  71.3 7.8 %collective-permute-start.6 = (f32[128,1,128]{2,1,0:T(1,128)S(1)}, f32[128,1,128]{2,1,0:T(1,128)S(1)}, u32[]{:S(2)}, u32[]{:S(2)}) collective-permute-start(f32[128,1,128]{2,1,0:T(1,128)S(1)} %get-tuple-element.33), channel_id=1, source_target_pairs={{0,32},{32,64},{64,96},{96,128},{128,160},{160,192},{192,224},{1,3... | collective-permute-start | bytes 196616 | tf_op jit(solution)/shard_map/ppermute | solution.py:33
  75.5 6.7 %collective-permute-start.7 = (f32[128,1,128]{2,1,0:T(1,128)S(1)}, f32[128,1,128]{2,1,0:T(1,128)S(1)}, u32[]{:S(2)}, u32[]{:S(2)}) collective-permute-start(f32[128,1,128]{2,1,0:T(1,128)S(1)} %get-tuple-element.34), channel_id=1, source_target_pairs={{32,0},{64,32},{96,64},{128,96},{160,128},{192,160},{224,192},{33,... | collective-permute-start | bytes 196616 | tf_op jit(solution)/shard_map/ppermute | solution.py:35
  88.4 8.8 %collective-permute-start.9 = (f32[128,18,1]{0,1,2:T(8,128)S(1)}, f32[128,18,1]{0,1,2:T(8,128)S(1)}, u32[]{:S(2)}, u32[]{:S(2)}) collective-permute-start(f32[128,18,1]{0,1,2:T(8,128)S(1)} %copy.89), channel_id=1, source_target_pairs={{0,1},{1,2},{2,3},{3,4},{4,5},{5,6},{6,7},{7,8},{8,9},{9,10},{10,1... | collective-permute-start | bytes 27656 | tf_op jit(solution)/shard_map/ppermute | solution.py:33
  88.5 7.0 %collective-permute-start.8 = (f32[128,18,1]{0,1,2:T(8,128)S(1)}, f32[128,18,1]{0,1,2:T(8,128)S(1)}, u32[]{:S(2)}, u32[]{:S(2)}) collective-permute-start(f32[128,18,1]{0,1,2:T(8,128)S(1)} %copy.87), channel_id=1, source_target_pairs={{1,0},{2,1},{3,2},{4,3},{5,4},{6,5},{7,6},{8,7},{9,8},{10,9},{11,1... | collective-permute-start | bytes 27656 | tf_op jit(solution)/shard_map/ppermute | solution.py:35
  98.8 4.2 %copy-start.14 = (f32[128,17,128]{2,1,0:T(8,128)S(1)}, f32[128,17,128]{2,1,0:T(8,128)}, u32[]{:S(2)}) copy-start(f32[128,17,128]{2,1,0:T(8,128)} %maximum_subtract_fusion.1) | copy-start | bytes 3342340
  103.1 7.8 %copy-start.16 = (bf16[512,2048]{1,0:T(8,128)(2,1)S(1)}, bf16[512,2048]{1,0:T(8,128)(2,1)}, u32[]{:S(2)}) copy-start(bf16[512,2048]{1,0:T(8,128)(2,1)} %copy-done.15) | copy-start | bytes 6291460
  103.1 7.9 %copy-start.24 = (bf16[128,2048]{0,1:T(8,128)(2,1)S(1)}, bf16[128,2048]{0,1:T(8,128)(2,1)}, u32[]{:S(2)}) copy-start(bf16[128,2048]{0,1:T(8,128)(2,1)} %copy-done.23) | copy-start | bytes 1572868
  105.5 6.8 %collective-permute-start.10 = (f32[128,1,128]{2,1,0:T(1,128)S(1)}, f32[128,1,128]{2,1,0:T(1,128)S(1)}, u32[]{:S(2)}, u32[]{:S(2)}) collective-permute-start(f32[128,1,128]{2,1,0:T(1,128)S(1)} %get-tuple-element.31), channel_id=1, source_target_pairs={{0,32},{32,64},{64,96},{96,128},{128,160},{160,192},{192,224},{1,3... | collective-permute-start | bytes 196616 | tf_op jit(solution)/shard_map/ppermute | solution.py:33
  109.5 8.5 %copy-start.10 = (f32[128,16,128]{2,1,0:T(8,128)S(1)}, f32[128,16,128]{2,1,0:T(8,128)}, u32[]{:S(2)}) copy-start(f32[128,16,128]{2,1,0:T(8,128)} %copy-done.9) | copy-start | bytes 3145732
  109.5 8.5 %collective-permute-start.11 = (f32[128,1,128]{2,1,0:T(1,128)S(1)}, f32[128,1,128]{2,1,0:T(1,128)S(1)}, u32[]{:S(2)}, u32[]{:S(2)}) collective-permute-start(f32[128,1,128]{2,1,0:T(1,128)S(1)} %get-tuple-element.32), channel_id=1, source_target_pairs={{32,0},{64,32},{96,64},{128,96},{160,128},{192,160},{224,192},{33,... | collective-permute-start | bytes 196616 | tf_op jit(solution)/shard_map/ppermute | solution.py:35
  122.3 7.1 %collective-permute-start.13 = (f32[128,18,1]{0,1,2:T(8,128)S(1)}, f32[128,18,1]{0,1,2:T(8,128)S(1)}, u32[]{:S(2)}, u32[]{:S(2)}) collective-permute-start(f32[128,18,1]{0,1,2:T(8,128)S(1)} %copy.93), channel_id=1, source_target_pairs={{0,1},{1,2},{2,3},{3,4},{4,5},{5,6},{6,7},{7,8},{8,9},{9,10},{10,1... | collective-permute-start | bytes 27656 | tf_op jit(solution)/shard_map/ppermute | solution.py:33
  122.4 5.2 %collective-permute-start.12 = (f32[128,18,1]{0,1,2:T(8,128)S(1)}, f32[128,18,1]{0,1,2:T(8,128)S(1)}, u32[]{:S(2)}, u32[]{:S(2)}) collective-permute-start(f32[128,18,1]{0,1,2:T(8,128)S(1)} %copy.91), channel_id=1, source_target_pairs={{1,0},{2,1},{3,2},{4,3},{5,4},{6,5},{7,6},{8,7},{9,8},{10,9},{11,1... | collective-permute-start | bytes 27656 | tf_op jit(solution)/shard_map/ppermute | solution.py:35
  134.9 250.2 %copy-start.1 = (bf16[512,512]{1,0:T(8,128)(2,1)S(1)}, bf16[512,512]{1,0:T(8,128)(2,1)}, u32[]{:S(2)}) copy-start(bf16[512,512]{1,0:T(8,128)(2,1)} %param.14) | copy-start | bytes 1572868
  (15 other events, 37.3 us)
Sparse Core Ops, SparseCore 0:
  112.5 267.8 all-reduce.2
where the time goes:
time: 400 us; the launch traced here: 392 us
  waiting for transfers between devices  253 us (63%)
  local copies, waits for them, and re-layouts  41.8 us (10%)
  other arithmetic  34 us (8%)
  starting transfers between devices  32.7 us (8%)
  matrix products  15.7 us (4%)
  between operations  14.8 us (4%)
    psum x1, waiting for transfers between devices, local(): lax.psum((term_first, term_second, term_third), ('lat', 'lon'))  243 us
    ppermute x6, starting transfers between devices, padded_2(): lax.ppermute(head, axis, [((i + 1) % count, i) for i in range(ends)])  15.3 us
    ppermute x6, starting transfers between devices, padded_2(): lax.ppermute(tail, axis, [(i, (i + 1) % count) for i in range(ends)])  13.8 us
    slice x6, local copies, waits for them, and re-layouts, padded_2(): head = lax.slice_in_dim(cells, 0, width, axis=dim)  11.7 us
    sub x3, other arithmetic, adjoint_step(): lon_diff = rows_mid[:, :, 1:] - rows_mid[:, :, :-1]  9.99 us
    ppermute x6, waiting for transfers between devices, padded_2(): lax.ppermute(head, axis, [((i + 1) % count, i) for i in range(ends)])  9.94 us
  transfers between devices with their start and end apart: 15, of which 4 were waited for; matrix products, arithmetic and copies ran while one was open for 16% of the time, Pallas kernels for 0%

commit v1 on v0

v1 whole, which is shorter than its diff:
```python
import functools
import math

import jax
import jax.numpy as jnp
from jax import lax
from jax.experimental import pallas as pl
from jax.experimental.pallas import tpu as pltpu
from jax.sharding import PartitionSpec as P

EPSILON = 1e-05
SUBSTEPS = 3
MESH = pl.DeviceIdType.MESH
BF = jnp.bfloat16
F32 = jnp.float32
LEV = 128
HID = 512
ROWS = 16
LON = 128
COLS = ROWS * LON
CHUNK_ROWS = 4
CHUNK = CHUNK_ROWS * LON
CHUNKS = ROWS // CHUNK_ROWS
PLANE = 16
DEPTH = 8
ROUNDS = ((4, 1, False), (0, 4, True), (5, 1, False))
FINISH_ROWS = 512


def dot(a, b):
    return jnp.dot(a, b, preferred_element_type=F32)


def dot_last(a, b):
    return lax.dot_general(a, b, (((1,), (1,)), ((), ())), preferred_element_type=F32)


def silu_and_slope(pre):
    sigma = 0.5 * jnp.tanh(0.5 * pre) + 0.5
    act = pre * sigma
    return act, sigma + act * (1.0 - sigma)


def place():
    lat, lon = lax.axis_index("lat"), lax.axis_index("lon")
    core = lax.rem(lon, 2)
    depth = lax.rem(lax.div(lon, 2), DEPTH)
    plane = lat * 2 + lax.div(lon, 16)
    return lat, lon, core, depth, plane


def loop(lo, hi, body):
    lax.fori_loop(lo, hi, lambda k, carry: (body(k), carry)[1], 0)


class Reduction:
    def __init__(self, part, plane_first, bufs, sems):
        self.part = part
        self.send0, self.recv0, self.half, self.send1, self.recv1, self.recv2, self.full = bufs
        (self.s0, self.r0, self.s1, self.r1, self.s2, self.r2, self.s3, self.r3, self.s4, self.r4) = sems
        lat, lon, self.core, depth, plane = place()
        self.sibling = (lat, lon + 1 - 2 * self.core)
        x, y = lax.rem(lat, 4), lax.div(lat, 4) * 2 + lax.div(lon, 16)
        planes, depths = [], []
        for kx, ky in sorted(((a, b) for a in range(4) for b in range(4) if a or b),
                             key=lambda k: -min(k[0], 4 - k[0]) - min(k[1], 4 - k[1])):
            to_x, to_y = lax.rem(x + kx, 4), lax.rem(y + ky, 4)
            to_lat, to_part = lax.div(to_y, 2) * 4 + to_x, lax.rem(to_y, 2)
            planes.append((to_lat * 2 + to_part, (to_lat, to_part * 16 + lax.rem(lon, 16))))
        for k in sorted(range(1, DEPTH), key=lambda k: -min(k, DEPTH - k)):
            to = lax.rem(depth + k, DEPTH)
            depths.append((to, (lat, lax.div(lon, 16) * 16 + to * 2 + self.core)))
        groups = ((plane, planes), (depth, depths))
        (self.me1, self.peers1), (self.me2, self.peers2) = groups if plane_first else groups[::-1]
        self.across = 4 if plane_first else 2

    def piece(self, index, base=0):
        width = HID // self.across
        row = pl.multiple_of(base + lax.div(index, self.across) * 16, 16)
        lane = pl.multiple_of(lax.rem(index, self.across) * width, width)
        return (slice(None), pl.ds(row, 16), pl.ds(lane, width))

    def copy0(self):
        return pltpu.make_async_remote_copy(
            src_ref=self.send0, dst_ref=self.recv0, send_sem=self.s0, recv_sem=self.r0,
            device_id=self.sibling, device_id_type=MESH)

    def copies1(self):
        return [pltpu.make_async_remote_copy(
            src_ref=self.send1.at[self.piece(to)], dst_ref=self.recv1.at[n],
            send_sem=self.s1.at[n], recv_sem=self.r1.at[n],
            device_id=device, device_id_type=MESH) for n, (to, device) in enumerate(self.peers1)]

    def copies2(self):
        mine = self.recv2.at[self.me2]
        return [pltpu.make_async_remote_copy(
            src_ref=mine, dst_ref=mine, send_sem=self.s2.at[n], recv_sem=self.r2.at[n],
            device_id=device, device_id_type=MESH) for n, (_, device) in enumerate(self.peers2)]

    def copies3(self):
        mine = self.full.at[self.piece(self.me1, 64 * self.core)]
        return [pltpu.make_async_remote_copy(
            src_ref=mine, dst_ref=mine, send_sem=self.s3.at[n], recv_sem=self.r3.at[n],
            device_id=device, device_id_type=MESH) for n, (_, device) in enumerate(self.peers1)]

    def copy4(self):
        mine = self.full.at[:, pl.ds(pl.multiple_of(64 * self.core, 64), 64), :]
        return pltpu.make_async_remote_copy(
            src_ref=mine, dst_ref=mine, send_sem=self.s4, recv_sem=self.r4,
            device_id=self.sibling, device_id_type=MESH)

    def step0(self):
        other = pl.multiple_of(64 * (1 - self.core), 64)
        self.send0[...] = self.part[:, pl.ds(other, 64), :].astype(BF)
        self.copy0().start()

    def step1(self):
        self.copy0().wait()
        mine = pl.multiple_of(64 * self.core, 64)
        self.half[...] = self.part[:, pl.ds(mine, 64), :] + self.recv0[...].astype(F32)
        self.send1[...] = self.half[...].astype(BF)
        for copy in self.copies1():
            copy.start()

    def step2(self):
        for copy in self.copies1():
            copy.wait()
        total = self.half[self.piece(self.me1)]
        for n in range(len(self.peers1)):
            total = total + self.recv1[n].astype(F32)
        self.recv2[self.me2] = total.astype(BF)
        for copy in self.copies2():
            copy.start()

    def step3(self):
        for copy in self.copies2():
            copy.wait()
        total = self.recv2[0].astype(F32)
        for n in range(1, len(self.peers2) + 1):
            total = total + self.recv2[n].astype(F32)
        self.full[self.piece(self.me1, 64 * self.core)] = total.astype(BF)
        for copy in self.copies3():
            copy.start()

    def step4(self):
        for copy in self.copies3():
            copy.wait()
        self.copy4().start()

    def finish(self):
        self.copy4().wait()


def kernel(scale, rounds, state_hbm, heat_hbm, scot_hbm, clon_hbm, clat_hbm, w1_hbm, w2_hbm, w3_hbm,
           out_hbm, first_hbm, second_hbm, third_hbm,
           nat_a, nat_b, state, heat, scot, clon, clat, w1, w2, w3, w1t, w2t, w3t,
           normed_s, inv_s, inputs_s, act1_s, slope1_s, back2_s, act2_s, part,
           cot_a, cot_b, high_s, low_s, sides_s, east_f, west_f, north_f, south_f, ends_f,
           shift_m, ends_m, pack_m, out_nat, first, second, third,
           rim_send, rim_recv, row_send, row_recv,
           load_sem, store_sem, rim_ss, rim_rs, row_ss, row_rs,
           *rest):
    lat, lon, core, depth, plane = place()
    lats, lons = lax.axis_size("lat"), lax.axis_size("lon")
    west_id = (lat, lax.rem(lon + lons - 1, lons))
    east_id = (lat, lax.rem(lon + 1, lons))
    up, down = lat < lats - 1, lat > 0
    reds = []
    for n, (lo, count, plane_first) in enumerate(rounds):
        own = rest[17 * n:17 * (n + 1)]
        reds.append(Reduction(part.at[pl.ds(lo, count)], plane_first, own[:7], own[7:]))
    early = reds[:-1]

    barrier = pltpu.get_barrier_semaphore()

    def greet(device):
        pl.semaphore_signal(barrier, inc=1, device_id=device, device_id_type=MESH)

    for _, device in reds[0].peers1 + reds[0].peers2:
        greet(device)
    greet(reds[0].sibling)
    greet(west_id)
    greet(east_id)

    loads = [pltpu.make_async_copy(src, dst, load_sem.at[i]) for i, (src, dst) in
             enumerate(((state_hbm, state), (w1_hbm, w1), (w2_hbm, w2), (w3_hbm, w3), (heat_hbm, heat),
                        (clon_hbm, clon), (clat_hbm, clat), (scot_hbm, scot)))]
    for load in loads:
        load.start()

    down_i = lax.broadcasted_iota(jnp.int32, (LEV, LON), 0)
    lane = lax.broadcasted_iota(jnp.int32, (LEV, LON), 1)
    for half in range(2):
        shift_m[half * LON:(half + 1) * LON, :LON] = (down_i == lane + 1).astype(BF)
        shift_m[half * LON:(half + 1) * LON, LON:] = (down_i + 1 == lane).astype(BF)
    for row in range(ROWS):
        cols = slice(row * LON, (row + 1) * LON)
        ends_m[:LON, cols] = jnp.where((down_i == 2 * row) & (lane == 0), 1.0, 0.0).astype(BF)
        ends_m[LON:, cols] = jnp.where(
            (down_i == 2 * row + 1) & (lane == LON - 1), 1.0, 0.0).astype(BF)
        pack_m[cols, :] = jnp.where(
            ((down_i == LON - 1) & (lane == 2 * row)) | ((down_i == 0) & (lane == 2 * row + 1)),
            1.0, 0.0).astype(BF)
    cot_a[0] = jnp.zeros((LEV, LON), F32)
    cot_b[0] = jnp.zeros((LEV, LON), F32)
    cot_a[ROWS + 1] = jnp.zeros((LEV, LON), F32)
    cot_b[ROWS + 1] = jnp.zeros((LEV, LON), F32)

    @pl.when(jnp.logical_not(down))
    def _():
        for slot in range(SUBSTEPS + 1):
            row_recv[slot, 0] = jnp.zeros((LEV, LON), BF)

    @pl.when(jnp.logical_not(up))
    def _():
        for slot in range(SUBSTEPS):
            row_recv[slot, 1] = jnp.zeros((LEV, LON), BF)

    for load in loads[:5]:
        load.wait()
    nat_a[...] = state[...].astype(F32)
    nat_b[...] = heat[...].astype(F32)
    w1t[...] = w1[...].T
    w2t[...] = w2[...].T
    w3t[...] = w3[...].T

    def rows_of(ref, first):
        return jnp.concatenate(
            [ref[pl.ds(first + i, LEV, stride=ROWS), :] for i in range(CHUNK_ROWS)], axis=1)

    blocks = [slice(128 * m, 128 * (m + 1)) for m in range(4)]

    def add_blocks(index, terms, new):
        for m in blocks:
            part[index, :, m] = terms[m, :] if new else part[index, :, m] + terms[m, :]

    def forward(chunk):
        cols = slice(chunk * CHUNK, (chunk + 1) * CHUNK)
        values = rows_of(nat_a, chunk * CHUNK_ROWS)
        inverse = lax.rsqrt(jnp.mean(values * values, axis=0, keepdims=True) + EPSILON)
        normed = values * inverse
        inputs = normed.astype(BF)
        normed_s[:, cols] = normed
        inv_s[:, cols] = inverse
        inputs_s[:, cols] = inputs
        cot = rows_of(nat_b, chunk * CHUNK_ROWS).astype(BF)
        act, slope = silu_and_slope(dot(w1[...], inputs))
        act1_s[:, cols] = act.astype(BF)
        slope1_s[:, cols] = slope
        act, slope = silu_and_slope(dot(w2[...], act1_s[:, cols]))
        act2_s[chunk % 2] = act.astype(BF)
        back2_s[:, cols] = (dot(w3t[...], cot) * slope).astype(BF)
        add_blocks(4, dot_last(act2_s[chunk % 2], cot), chunk == 0)
        terms = dot_last(back2_s[:, cols], act1_s[:, cols]).reshape(4, 128, HID)
        part[:4] = terms if chunk == 0 else part[:4] + terms

    for chunk in range(CHUNKS):
        forward(chunk)
    pl.semaphore_wait(barrier, (PLANE - 1) + (DEPTH - 1) + 3)
    for red in early:
        red.step0()

    def rim_copy(slot, way):
        return pltpu.make_async_remote_copy(
            src_ref=rim_send.at[slot], dst_ref=rim_recv.at[slot, way],
            send_sem=rim_ss.at[slot, way], recv_sem=rim_rs.at[slot, way],
            device_id=(east_id, west_id)[way], device_id_type=MESH)

    def row_copy(slot, way):
        return pltpu.make_async_remote_copy(
            src_ref=row_send.at[slot, way], dst_ref=row_recv.at[slot, way],
            send_sem=row_ss.at[slot, way], recv_sem=row_rs.at[slot, way],
            device_id=(jnp.clip(lat + (1, -1)[way], 0, lats - 1), lon), device_id_type=MESH)

    def send_rows(slot, ways):
        for way in ways:
            pl.when((up, down)[way])(lambda: row_copy(slot, way).start())

    def wait_rows(slot, ways):
        for way in ways:
            pl.when((up, down)[way])(lambda: row_copy(slot, way).wait_send())
            pl.when((down, up)[way])(lambda: row_copy(slot, way).wait_recv())

    def backward(chunk):
        cols = slice(chunk * CHUNK, (chunk + 1) * CHUNK)
        back = (dot(w2t[...], back2_s[:, cols]) * slope1_s[:, cols]).astype(BF)
        act2_s[chunk % 2] = back
        add_blocks(5, dot_last(back, inputs_s[:, cols]), chunk == 0)
        input_cot = dot(w1t[...], act2_s[chunk % 2])
        normed = normed_s[:, cols]
        state_part = inv_s[:, cols] * (
            input_cot - normed * jnp.mean(input_cot * normed, axis=0, keepdims=True))
        for i in range(CHUNK_ROWS):
            row = chunk * CHUNK_ROWS + i
            keep(row, state_part[:, i * LON:(i + 1) * LON] + scot[pl.ds(row, LEV, stride=ROWS), :],
                 cot_a)

    def keep(row, new, cells):
        cells[row + 1] = new
        high = new.astype(BF)
        high_s[row] = high
        low_s[row] = (new - high.astype(F32)).astype(BF)

    def packed():
        return sum(dot(jnp.concatenate([high_s[row], high_s[row + 1]], axis=1),
                       pack_m[row * LON:(row + 2) * LON, :]) for row in range(0, ROWS, 2)).astype(BF)

    loads[7].wait()
    for chunk in range(CHUNKS // 2):
        backward(chunk)
    for red in early:
        red.step1()
    for chunk in range(CHUNKS // 2, CHUNKS):
        backward(chunk)
    reds[-1].step0()

    def send_halo(slot):
        row_send[slot, 0] = high_s[ROWS - 1]
        row_send[slot, 1] = high_s[0]
        send_rows(slot, (0, 1))
        rim_send[slot] = packed()
        rim_copy(slot, 0).start()
        rim_copy(slot, 1).start()

    loads[5].wait()
    loads[6].wait()
    nat_a[...] = clon[...].astype(F32)
    nat_b[...] = clat[...].astype(F32)
    row_send[SUBSTEPS, 0] = nat_b[pl.ds(ROWS - 1, LEV, stride=ROWS), :].astype(BF)
    send_rows(SUBSTEPS, (0,))
    faces_pairs = [jnp.concatenate(
        [nat_a[pl.ds(row + i, LEV, stride=ROWS), :].astype(BF) for i in range(2)], axis=1)
        for row in range(0, ROWS, 2)]
    rim_send[SUBSTEPS] = sum(dot(pair, pack_m[2 * i * LON:2 * (i + 1) * LON, :])
                             for i, pair in enumerate(faces_pairs)).astype(BF)
    rim_copy(SUBSTEPS, 0).start()
    send_halo(0)
    reds[-1].step1()

    def sides():
        sides_s[...] = dot(jnp.concatenate(
            [high_s[...].reshape(COLS, LON), low_s[...].reshape(COLS, LON)], axis=1), shift_m[...])

    sides()

    def split_lat(row):
        ahead = nat_b[pl.ds(row, LEV, stride=ROWS), :]
        north_f[row] = jnp.maximum(ahead, 0.0)
        south_f[row + 1] = jnp.minimum(ahead, 0.0)

    loop(0, ROWS, split_lat)
    rim_copy(SUBSTEPS, 0).wait()
    wait_rows(SUBSTEPS, (0,))
    south_f[0] = jnp.minimum(row_recv[SUBSTEPS, 0].astype(F32), 0.0)
    west_rim = rim_recv[SUBSTEPS, 0]
    for row in range(ROWS):
        faces = nat_a[pl.ds(row, LEV, stride=ROWS), :]
        west = dot(jnp.concatenate([faces.astype(BF), west_rim], axis=1), jnp.concatenate(
            [shift_m[:LON, LON:], ends_m[:LON, row * LON:(row + 1) * LON]], axis=0))
        west = jnp.minimum(west, 0.0)
        faces = jnp.maximum(faces, 0.0)
        east_f[row] = faces
        west_f[row] = west
        ends_f[row] = jnp.where(lane == LON - 1, faces, jnp.where(lane == 0, -west, 0.0))

    def inner(cells, new_cells):
        def one_row(row):
            centre = cells[row + 1]
            here = pl.ds(pl.multiple_of(row * LEV, LEV), LEV)
            new_cells[row + 1] = (
                centre + east_f[row] * (sides_s[here, :LON] - centre)
                + west_f[row] * (centre - sides_s[here, LON:])
                + north_f[row] * (cells[row + 2] - centre)
                + south_f[row] * (centre - cells[row]))

        loop(0, ROWS, one_row)

    def outer(slot, new_cells, store):
        rim_copy(slot, 0).wait()
        rim_copy(slot, 1).wait()
        wait_rows(slot, (0, 1))
        rims = jnp.concatenate([rim_recv[slot, 0], rim_recv[slot, 1]], axis=1)
        for row in range(0, ROWS, 2):
            ends = dot(rims, ends_m[:, row * LON:(row + 2) * LON])
            for i in range(2):
                new = new_cells[row + i + 1] + ends_f[row + i] * ends[:, i * LON:(i + 1) * LON]
                if row + i == 0:
                    new = new - south_f[0] * row_recv[slot, 0].astype(F32)
                if row + i == ROWS - 1:
                    new = new + north_f[ROWS - 1] * row_recv[slot, 1].astype(F32)
                store(row + i, new, new_cells)

    def into_natural(row, new, cells):
        out_nat[pl.ds(row, LEV, stride=ROWS), :] = new

    stores = [pltpu.make_async_copy(src, dst, store_sem.at[i]) for i, (src, dst) in enumerate(
        ((out_nat, out_hbm), (first, first_hbm), (second, second_hbm), (third, third_hbm)))]

    third_red, second_red, first_red = reds
    inner(cot_a, cot_b)
    third_red.step2()
    second_red.step2()
    outer(0, cot_b, keep)
    send_halo(1)
    first_red.step2()
    sides()
    inner(cot_b, cot_a)
    third_red.step3()
    outer(1, cot_a, keep)
    send_halo(2)
    sides()
    inner(cot_a, cot_b)
    second_red.step3()
    first_red.step3()
    third_red.step4()
    outer(2, cot_b, into_natural)
    stores[0].start()
    first_red.step4()
    second_red.step4()
    third_red.finish()

    def total(index):
        for (lo, count, _), red in zip(rounds, reds):
            if lo <= index < lo + count:
                return red.full[index - lo].astype(F32) * scale

    sum_third = total(4)
    for m in blocks:
        third[:, m] = sum_third[:, m].T
    stores[3].start()
    first_red.finish()
    sum_first = total(5)
    for m in blocks:
        first[m, :] = sum_first[:, m]
    stores[1].start()
    second_red.finish()
    for i, m in enumerate(blocks):
        second[m, :] = total(i)
    stores[2].start()
    for store in stores:
        store.wait()


def reduction_scratch(nb, plane_first):
    n1, n2 = (PLANE, DEPTH) if plane_first else (DEPTH, PLANE)
    width = HID * 4 // n1
    half, piece = (nb, 64, HID), (nb, 16, width)
    bufs = [
        pltpu.VMEM(half, BF), pltpu.VMEM(half, BF), pltpu.VMEM(half, F32), pltpu.VMEM(half, BF),
        pltpu.VMEM((n1 - 1,) + piece, BF), pltpu.VMEM((n2,) + piece, BF), pltpu.VMEM((nb, 128, HID), BF),
    ]
    dma = pltpu.SemaphoreType.DMA
    sems = [dma, dma, dma((n1 - 1,)), dma((n1 - 1,)), dma((n2 - 1,)), dma((n2 - 1,)),
            dma((n1 - 1,)), dma((n1 - 1,)), dma, dma]
    return bufs + sems


def finish_kernel(*refs):
    ins, outs, held, load_sem, store_sem = refs[:4], refs[4:8], refs[8:12], refs[12], refs[13]
    moves = []
    for src, dst, buf in zip(ins, outs, held):
        size = min(src.shape[0], FINISH_ROWS * 128 // src.shape[1])
        for first in range(0, src.shape[0], size):
            rows = pl.ds(first, size)
            n = len(moves)
            moves.append((
                pltpu.make_async_copy(src.at[rows], buf.at[rows], load_sem.at[n]),
                pltpu.make_async_copy(buf.at[rows], dst.at[rows], store_sem.at[n])))
    for load, _ in moves:
        load.start()
    for load, store in moves:
        load.wait()
        store.start()
    for _, store in moves:
        store.wait()


def local(state, heat_cot, state_cot, courant_lon, courant_lat, w_first, w_second, w_third):
    levels, lat_rows, lon_cols = state.shape
    scale = 1.0 / math.sqrt(lat_rows * lon_cols * lax.axis_size("lat") * lax.axis_size("lon"))
    flat = (levels * lat_rows, lon_cols)
    hbm = pl.BlockSpec(memory_space=pl.ANY)
    dma = pltpu.SemaphoreType.DMA
    tile = (LEV, LON)
    bfs = lambda *shapes: [pltpu.VMEM(shape, BF) for shape in shapes]
    f32s = lambda *shapes: [pltpu.VMEM(shape, F32) for shape in shapes]
    grid = (ROWS,) + tile
    halo = (SUBSTEPS + 1, 2)
    scratch = [
        *f32s(flat, flat), *bfs(flat, flat), *f32s(flat), *bfs(flat, flat),
        *bfs((HID, LEV), (HID, HID), (LEV, HID), (LEV, HID), (HID, HID), (HID, LEV)),
        *f32s((LEV, COLS), (1, COLS)), *bfs((LEV, COLS), (HID, COLS)), *f32s((HID, COLS)),
        *bfs((HID, COLS), (2, HID, CHUNK)), *f32s((6, 128, 512)),
        *f32s((ROWS + 2,) + tile, (ROWS + 2,) + tile), *bfs(grid, grid), *f32s((COLS, 2 * LON)),
        *f32s(grid, grid, grid, (ROWS + 1,) + tile, grid),
        *bfs((2 * LON, 2 * LON), (2 * LON, COLS), (COLS, LON)),
        *f32s(flat, (HID, LEV), (HID, HID), (LEV, HID)),
        *bfs((SUBSTEPS + 1,) + tile, halo + tile, halo + tile, halo + tile),
        dma((8,)), dma((4,)), dma(halo), dma(halo), dma(halo), dma(halo),
    ]
    for _, count, plane_first in ROUNDS:
        scratch += reduction_scratch(count, plane_first)
    shapes = (flat, (HID, LEV), (HID, HID), (LEV, HID))
    results = tuple(jax.ShapeDtypeStruct(shape, F32) for shape in shapes)
    out = pl.pallas_call(
        functools.partial(kernel, scale, ROUNDS),
        out_shape=results,
        in_specs=[hbm] * 8,
        out_specs=(hbm,) * 4,
        scratch_shapes=scratch,
        compiler_params=pltpu.CompilerParams(
            collective_id=0, has_side_effects=True, vmem_limit_bytes=60 << 20),
    )(state.reshape(flat), heat_cot.reshape(flat), state_cot.reshape(flat),
      courant_lon.reshape(flat), courant_lat.reshape(flat), w_first, w_second, w_third)
    grid, first, second, third = pl.pallas_call(
        finish_kernel, out_shape=results, in_specs=[hbm] * 4, out_specs=(hbm,) * 4,
        scratch_shapes=[*f32s(*shapes), dma((16,)), dma((16,))],
        compiler_params=pltpu.CompilerParams(vmem_limit_bytes=60 << 20),
    )(*out)
    return grid.reshape(state.shape), first, second, third


def solution(mesh):
    split = P(None, "lat", "lon")
    return jax.shard_map(
        local, mesh=mesh, in_specs=(split,) * 5 + (P(),) * 3,
        out_specs=(split, P(), P(), P()), check_vma=False)
```

time: 400 us -> 44.7 us (0.11)
  the two profiles are of different devices: /device:TPU:8 before, /device:TPU:1 now
where the time goes in v1:
time: 44.7 us; the launch traced here: 44.6 us
  Pallas kernels  43.8 us (98%)
  between operations  0.8 us (2%)
    pallas_call x1, Pallas kernels, local(): pl.pallas_call(functools.partial(kernel, scale, ROUNDS), out_shape=result...  41.1 us
    pallas_call x1, Pallas kernels, local(): pl.pallas_call(finish_kernel, out_shape=results, in_specs=[hbm] * 4, out_...  2.71 us

profile of v1, /device:TPU:1, one launch (start us, length us, event | category | flops | bytes accessed | tf_op | source)
XLA Modules:
  0.0 44.6 jit_solution(17361067154556467647)
XLA Ops:
  0.6 41.1 %shard_map.111 = (f32[2048,128]{1,0:T(8,128)}, f32[512,128]{1,0:T(8,128)}, f32[512,512]{1,0:T(8,128)}, f32[128,512]{1,0:T(8,128)}) custom-call(bf16[2048,128]{1,0:T(8,128)(2,1)} %bitcast.7, bf16[2048,128]{1,0:T(8,128)(2,1)} %bitcast.8, f32[2048,128]{1,0:T(8,128)} %bitcast.6, bf16[2048,128]{1,0:T(8,128)(2,1)} %bitcast.9, bf16[2048,128]{1,0:T(8,128)(2,1)} %bitcast.10, ...), custom_call_target="tpu_custom_call" | custom-call | tf_op jit(solution)/shard_map/pallas_call | solution.py:505
  41.7 2.7 %shard_map.112 = (f32[2048,128]{1,0:T(8,128)}, f32[512,128]{1,0:T(8,128)}, f32[512,512]{1,0:T(8,128)}, f32[128,512]{1,0:T(8,128)}) custom-call(f32[2048,128]{1,0:T(8,128)} %get-tuple-element.12.refs_0_, f32[512,128]{1,0:T(8,128)} %get-tuple-element.13.refs_1_, f32[512,512]{1,0:T(8,128)} %get-tuple-element.14.refs_2_, f32[128,512]{1,0:T(8,128)} %get-tuple-element.15.refs_3_), custom_call_target="tpu_custom_call" | custom-call | tf_op jit(solution)/shard_map/pallas_call | solution.py:515

commit v2 on v1

--- a/solution.py
+++ b/solution.py
@@ -18,12 +18,12 @@
 ROWS = 16
 LON = 128
 COLS = ROWS * LON
-CHUNK_ROWS = 4
+CHUNK_ROWS = 8
 CHUNK = CHUNK_ROWS * LON
 CHUNKS = ROWS // CHUNK_ROWS
 PLANE = 16
 DEPTH = 8
-ROUNDS = ((4, 1, False), (0, 4, True), (5, 1, False))
+ROUNDS = ((0, 2, True), (2, 2, True), (4, 1, False), (5, 1, False))
 FINISH_ROWS = 512
 
 
@@ -154,7 +154,7 @@
 def kernel(scale, rounds, state_hbm, heat_hbm, scot_hbm, clon_hbm, clat_hbm, w1_hbm, w2_hbm, w3_hbm,
            out_hbm, first_hbm, second_hbm, third_hbm,
            nat_a, nat_b, state, heat, scot, clon, clat, w1, w2, w3, w1t, w2t, w3t,
-           normed_s, inv_s, inputs_s, act1_s, slope1_s, back2_s, act2_s, part,
+           normed_s, inv_s, inputs_s, act1_s, slope1_s, back2_s, act2_s, back1_s, part,
            cot_a, cot_b, high_s, low_s, sides_s, east_f, west_f, north_f, south_f, ends_f,
            shift_m, ends_m, pack_m, out_nat, first, second, third,
            rim_send, rim_recv, row_send, row_recv,
@@ -169,7 +169,7 @@
     for n, (lo, count, plane_first) in enumerate(rounds):
         own = rest[17 * n:17 * (n + 1)]
         reds.append(Reduction(part.at[pl.ds(lo, count)], plane_first, own[:7], own[7:]))
-    early = reds[:-1]
+    left_red, right_red, third_red, first_red = reds
 
     barrier = pltpu.get_barrier_semaphore()
 
@@ -230,9 +230,19 @@
 
     blocks = [slice(128 * m, 128 * (m + 1)) for m in range(4)]
 
+    halves = [slice(256 * m, 256 * (m + 1)) for m in range(2)]
+
+    def add(here, terms, new):
+        part[here] = terms if new else part[here] + terms
+
     def add_blocks(index, terms, new):
         for m in blocks:
-            part[index, :, m] = terms[m, :] if new else part[index, :, m] + terms[m, :]
+            add((index, slice(None), m), terms[m, :], new)
+
+    def add_second(terms, new):
+        for n in range(8):
+            side, i, j = n // 4, n // 2 % 2, n % 2
+            add((2 * side + i, slice(None), halves[j]), terms[blocks[2 * i + j], halves[side]], new)
 
     def forward(chunk):
         cols = slice(chunk * CHUNK, (chunk + 1) * CHUNK)
@@ -248,17 +258,17 @@
         act1_s[:, cols] = act.astype(BF)
         slope1_s[:, cols] = slope
         act, slope = silu_and_slope(dot(w2[...], act1_s[:, cols]))
-        act2_s[chunk % 2] = act.astype(BF)
+        act2_s[:, cols] = act.astype(BF)
         back2_s[:, cols] = (dot(w3t[...], cot) * slope).astype(BF)
-        add_blocks(4, dot_last(act2_s[chunk % 2], cot), chunk == 0)
-        terms = dot_last(back2_s[:, cols], act1_s[:, cols]).reshape(4, 128, HID)
-        part[:4] = terms if chunk == 0 else part[:4] + terms
+        add_blocks(4, dot_last(act2_s[:, cols], cot), chunk == 0)
+        add_second(dot_last(back2_s[:, cols], act1_s[:, cols]), chunk == 0)
 
     for chunk in range(CHUNKS):
         forward(chunk)
     pl.semaphore_wait(barrier, (PLANE - 1) + (DEPTH - 1) + 3)
-    for red in early:
-        red.step0()
+    left_red.step0()
+    right_red.step0()
+    third_red.step0()
 
     def rim_copy(slot, way):
         return pltpu.make_async_remote_copy(
@@ -283,10 +293,12 @@
 
     def backward(chunk):
         cols = slice(chunk * CHUNK, (chunk + 1) * CHUNK)
-        back = (dot(w2t[...], back2_s[:, cols]) * slope1_s[:, cols]).astype(BF)
-        act2_s[chunk % 2] = back
-        add_blocks(5, dot_last(back, inputs_s[:, cols]), chunk == 0)
-        input_cot = dot(w1t[...], act2_s[chunk % 2])
+        back1_s[:, cols] = (dot(w2t[...], back2_s[:, cols]) * slope1_s[:, cols]).astype(BF)
+        add_blocks(5, dot_last(back1_s[:, cols], inputs_s[:, cols]), chunk == 0)
+
+    def input_part(chunk):
+        cols = slice(chunk * CHUNK, (chunk + 1) * CHUNK)
+        input_cot = dot(w1t[...], back1_s[:, cols])
         normed = normed_s[:, cols]
         state_part = inv_s[:, cols] * (
             input_cot - normed * jnp.mean(input_cot * normed, axis=0, keepdims=True))
@@ -305,14 +317,16 @@
         return sum(dot(jnp.concatenate([high_s[row], high_s[row + 1]], axis=1),
                        pack_m[row * LON:(row + 2) * LON, :]) for row in range(0, ROWS, 2)).astype(BF)
 
+    backward(0)
+    left_red.step1()
+    backward(1)
+    right_red.step1()
+    third_red.step1()
+    first_red.step0()
     loads[7].wait()
-    for chunk in range(CHUNKS // 2):
-        backward(chunk)
-    for red in early:
-        red.step1()
-    for chunk in range(CHUNKS // 2, CHUNKS):
-        backward(chunk)
-    reds[-1].step0()
+    for chunk in range(CHUNKS):
+        input_part(chunk)
+    first_red.step1()
 
     def send_halo(slot):
         row_send[slot, 0] = high_s[ROWS - 1]
@@ -335,7 +349,6 @@
                              for i, pair in enumerate(faces_pairs)).astype(BF)
     rim_copy(SUBSTEPS, 0).start()
     send_halo(0)
-    reds[-1].step1()
 
     def sides():
         sides_s[...] = dot(jnp.concatenate(
@@ -396,47 +409,48 @@
     stores = [pltpu.make_async_copy(src, dst, store_sem.at[i]) for i, (src, dst) in enumerate(
         ((out_nat, out_hbm), (first, first_hbm), (second, second_hbm), (third, third_hbm)))]
 
-    third_red, second_red, first_red = reds
     inner(cot_a, cot_b)
     third_red.step2()
-    second_red.step2()
+    left_red.step2()
+    right_red.step2()
     outer(0, cot_b, keep)
     send_halo(1)
     first_red.step2()
     sides()
     inner(cot_b, cot_a)
     third_red.step3()
+    left_red.step3()
     outer(1, cot_a, keep)
     send_halo(2)
     sides()
     inner(cot_a, cot_b)
-    second_red.step3()
+    right_red.step3()
     first_red.step3()
     third_red.step4()
+    left_red.step4()
     outer(2, cot_b, into_natural)
     stores[0].start()
+    third_red.finish()
+    for m in blocks:
+        third[:, m] = (third_red.full[0, :, m].astype(F32) * scale).T
+    stores[3].start()
+
+    def put_second(red, side):
+        for i in range(2):
+            for j, m in enumerate(halves):
+                second[blocks[2 * i + j], side] = red.full[i, :, m].astype(F32) * scale
+
+    right_red.step4()
     first_red.step4()
-    second_red.step4()
-    third_red.finish()
-
-    def total(index):
-        for (lo, count, _), red in zip(rounds, reds):
-            if lo <= index < lo + count:
-                return red.full[index - lo].astype(F32) * scale
-
-    sum_third = total(4)
+    left_red.finish()
+    put_second(left_red, halves[0])
+    right_red.finish()
+    put_second(right_red, halves[1])
+    stores[2].start()
+    first_red.finish()
     for m in blocks:
-        third[:, m] = sum_third[:, m].T
-    stores[3].start()
-    first_red.finish()
-    sum_first = total(5)
-    for m in blocks:
-        first[m, :] = sum_first[:, m]
+        first[m, :] = first_red.full[0, :, m].astype(F32) * scale
     stores[1].start()
-    second_red.finish()
-    for i, m in enumerate(blocks):
-        second[m, :] = total(i)
-    stores[2].start()
     for store in stores:
         store.wait()
 
@@ -490,7 +504,7 @@
         *f32s(flat, flat), *bfs(flat, flat), *f32s(flat), *bfs(flat, flat),
         *bfs((HID, LEV), (HID, HID), (LEV, HID), (LEV, HID), (HID, HID), (HID, LEV)),
         *f32s((LEV, COLS), (1, COLS)), *bfs((LEV, COLS), (HID, COLS)), *f32s((HID, COLS)),
-        *bfs((HID, COLS), (2, HID, CHUNK)), *f32s((6, 128, 512)),
+        *bfs((HID, COLS), (HID, COLS), (HID, COLS)), *f32s((6, 128, 512)),
         *f32s((ROWS + 2,) + tile, (ROWS + 2,) + tile), *bfs(grid, grid), *f32s((COLS, 2 * LON)),
         *f32s(grid, grid, grid, (ROWS + 1,) + tile, grid),
         *bfs((2 * LON, 2 * LON), (2 * LON, COLS), (COLS, LON)),

time: 44.7 us -> 46.3 us (1.036)
  Pallas kernels: 43.8 us -> 45.3 us
    pallas_call x1, Pallas kernels: 41.1 us -> 42.6 us  [local(): pl.pallas_call(functools.partial(kernel, scale, ROUNDS), out_shape=result...]
where the time goes in v2:
time: 46.3 us; the launch traced here: 46.1 us
  Pallas kernels  45.3 us (98%)
  between operations  0.8 us (2%)
    pallas_call x1, Pallas kernels, local(): pl.pallas_call(functools.partial(kernel, scale, ROUNDS), out_shape=result...  42.6 us
    pallas_call x1, Pallas kernels, local(): pl.pallas_call(finish_kernel, out_shape=results, in_specs=[hbm] * 4, out_...  2.71 us

profile of v2, /device:TPU:1, one launch (start us, length us, event | category | flops | bytes accessed | tf_op | source)
XLA Modules:
  0.0 46.1 jit_solution(6348622341334308720)
XLA Ops:
  0.6 42.6 %shard_map.111 = (f32[2048,128]{1,0:T(8,128)}, f32[512,128]{1,0:T(8,128)}, f32[512,512]{1,0:T(8,128)}, f32[128,512]{1,0:T(8,128)}) custom-call(bf16[2048,128]{1,0:T(8,128)(2,1)} %bitcast.7, bf16[2048,128]{1,0:T(8,128)(2,1)} %bitcast.8, f32[2048,128]{1,0:T(8,128)} %bitcast.6, bf16[2048,128]{1,0:T(8,128)(2,1)} %bitcast.9, bf16[2048,128]{1,0:T(8,128)(2,1)} %bitcast.10, ...), custom_call_target="tpu_custom_call" | custom-call | tf_op jit(solution)/shard_map/pallas_call | solution.py:519
  43.3 2.7 %shard_map.112 = (f32[2048,128]{1,0:T(8,128)}, f32[512,128]{1,0:T(8,128)}, f32[512,512]{1,0:T(8,128)}, f32[128,512]{1,0:T(8,128)}) custom-call(f32[2048,128]{1,0:T(8,128)} %get-tuple-element.12.refs_0_, f32[512,128]{1,0:T(8,128)} %get-tuple-element.13.refs_1_, f32[512,512]{1,0:T(8,128)} %get-tuple-element.14.refs_2_, f32[128,512]{1,0:T(8,128)} %get-tuple-element.15.refs_3_), custom_call_target="tpu_custom_call" | custom-call | tf_op jit(solution)/shard_map/pallas_call | solution.py:529

commit v3 on v1

--- a/solution.py
+++ b/solution.py
@@ -88,20 +88,25 @@
     def copies1(self):
         return [pltpu.make_async_remote_copy(
             src_ref=self.send1.at[self.piece(to)], dst_ref=self.recv1.at[n],
-            send_sem=self.s1.at[n], recv_sem=self.r1.at[n],
+            send_sem=self.s1, recv_sem=self.r1,
             device_id=device, device_id_type=MESH) for n, (to, device) in enumerate(self.peers1)]
 
     def copies2(self):
         mine = self.recv2.at[self.me2]
         return [pltpu.make_async_remote_copy(
-            src_ref=mine, dst_ref=mine, send_sem=self.s2.at[n], recv_sem=self.r2.at[n],
-            device_id=device, device_id_type=MESH) for n, (_, device) in enumerate(self.peers2)]
+            src_ref=mine, dst_ref=mine, send_sem=self.s2, recv_sem=self.r2,
+            device_id=device, device_id_type=MESH) for _, device in self.peers2]
 
     def copies3(self):
         mine = self.full.at[self.piece(self.me1, 64 * self.core)]
         return [pltpu.make_async_remote_copy(
-            src_ref=mine, dst_ref=mine, send_sem=self.s3.at[n], recv_sem=self.r3.at[n],
-            device_id=device, device_id_type=MESH) for n, (_, device) in enumerate(self.peers1)]
+            src_ref=mine, dst_ref=mine, send_sem=self.s3, recv_sem=self.r3,
+            device_id=device, device_id_type=MESH) for _, device in self.peers1]
+
+    def all_of(self, ref, send_sem, recv_sem):
+        return pltpu.make_async_remote_copy(
+            src_ref=ref, dst_ref=ref, send_sem=send_sem, recv_sem=recv_sem,
+            device_id=self.sibling, device_id_type=MESH)
 
     def copy4(self):
         mine = self.full.at[:, pl.ds(pl.multiple_of(64 * self.core, 64), 64), :]
@@ -123,8 +128,7 @@
             copy.start()
 
     def step2(self):
-        for copy in self.copies1():
-            copy.wait()
+        self.all_of(self.recv1, self.s1, self.r1).wait()
         total = self.half[self.piece(self.me1)]
         for n in range(len(self.peers1)):
             total = total + self.recv1[n].astype(F32)
@@ -133,8 +137,7 @@
             copy.start()
 
     def step3(self):
-        for copy in self.copies2():
-            copy.wait()
+        self.all_of(self.recv2.at[pl.ds(0, len(self.peers2))], self.s2, self.r2).wait()
         total = self.recv2[0].astype(F32)
         for n in range(1, len(self.peers2) + 1):
             total = total + self.recv2[n].astype(F32)
@@ -143,8 +146,7 @@
             copy.start()
 
     def step4(self):
-        for copy in self.copies3():
-            copy.wait()
+        self.all_of(self.recv1, self.s3, self.r3).wait()
         self.copy4().start()
 
     def finish(self):
@@ -450,9 +452,7 @@
         pltpu.VMEM((n1 - 1,) + piece, BF), pltpu.VMEM((n2,) + piece, BF), pltpu.VMEM((nb, 128, HID), BF),
     ]
     dma = pltpu.SemaphoreType.DMA
-    sems = [dma, dma, dma((n1 - 1,)), dma((n1 - 1,)), dma((n2 - 1,)), dma((n2 - 1,)),
-            dma((n1 - 1,)), dma((n1 - 1,)), dma, dma]
-    return bufs + sems
+    return bufs + [dma] * 10
 
 
 def finish_kernel(*refs):

time: 44.7 us -> 43 us (0.962)
  Pallas kernels: 43.8 us -> 42.1 us
    pallas_call x1, Pallas kernels: 41.1 us -> 39.4 us  [local(): pl.pallas_call(functools.partial(kernel, scale, ROUNDS), out_shape=result...]
where the time goes in v3:
time: 43 us; the launch traced here: 42.9 us
  Pallas kernels  42.1 us (98%)
  between operations  0.8 us (2%)
    pallas_call x1, Pallas kernels, local(): pl.pallas_call(functools.partial(kernel, scale, ROUNDS), out_shape=result...  39.4 us
    pallas_call x1, Pallas kernels, local(): pl.pallas_call(finish_kernel, out_shape=results, in_specs=[hbm] * 4, out_...  2.71 us

profile of v3, /device:TPU:1, one launch (start us, length us, event | category | flops | bytes accessed | tf_op | source)
XLA Modules:
  0.0 42.9 jit_solution(3671179197459595912)
XLA Ops:
  0.6 39.4 %shard_map.111 = (f32[2048,128]{1,0:T(8,128)}, f32[512,128]{1,0:T(8,128)}, f32[512,512]{1,0:T(8,128)}, f32[128,512]{1,0:T(8,128)}) custom-call(bf16[2048,128]{1,0:T(8,128)(2,1)} %bitcast.7, bf16[2048,128]{1,0:T(8,128)(2,1)} %bitcast.8, f32[2048,128]{1,0:T(8,128)} %bitcast.6, bf16[2048,128]{1,0:T(8,128)(2,1)} %bitcast.9, bf16[2048,128]{1,0:T(8,128)(2,1)} %bitcast.10, ...), custom_call_target="tpu_custom_call" | custom-call | tf_op jit(solution)/shard_map/pallas_call | solution.py:505
  40.0 2.7 %shard_map.112 = (f32[2048,128]{1,0:T(8,128)}, f32[512,128]{1,0:T(8,128)}, f32[512,512]{1,0:T(8,128)}, f32[128,512]{1,0:T(8,128)}) custom-call(f32[2048,128]{1,0:T(8,128)} %get-tuple-element.12.refs_0_, f32[512,128]{1,0:T(8,128)} %get-tuple-element.13.refs_1_, f32[512,512]{1,0:T(8,128)} %get-tuple-element.14.refs_2_, f32[128,512]{1,0:T(8,128)} %get-tuple-element.15.refs_3_), custom_call_target="tpu_custom_call" | custom-call | tf_op jit(solution)/shard_map/pallas_call | solution.py:515

commit v4 on v3

--- a/solution.py
+++ b/solution.py
@@ -156,11 +156,11 @@
 def kernel(scale, rounds, state_hbm, heat_hbm, scot_hbm, clon_hbm, clat_hbm, w1_hbm, w2_hbm, w3_hbm,
            out_hbm, first_hbm, second_hbm, third_hbm,
            nat_a, nat_b, state, heat, scot, clon, clat, w1, w2, w3, w1t, w2t, w3t,
-           normed_s, inv_s, inputs_s, act1_s, slope1_s, back2_s, act2_s, part,
+           normed_s, inv_s, inputs_s, act1_s, slope1_s, back2_s, act2_s, back1_s, part,
            cot_a, cot_b, high_s, low_s, sides_s, east_f, west_f, north_f, south_f, ends_f,
            shift_m, ends_m, pack_m, out_nat, first, second, third,
            rim_send, rim_recv, row_send, row_recv,
-           load_sem, store_sem, rim_ss, rim_rs, row_ss, row_rs,
+           load_sem, store_sem, second_sem, rim_ss, rim_rs, row_ss, row_rs,
            *rest):
     lat, lon, core, depth, plane = place()
     lats, lons = lax.axis_size("lat"), lax.axis_size("lon")
@@ -285,10 +285,12 @@
 
     def backward(chunk):
         cols = slice(chunk * CHUNK, (chunk + 1) * CHUNK)
-        back = (dot(w2t[...], back2_s[:, cols]) * slope1_s[:, cols]).astype(BF)
-        act2_s[chunk % 2] = back
-        add_blocks(5, dot_last(back, inputs_s[:, cols]), chunk == 0)
-        input_cot = dot(w1t[...], act2_s[chunk % 2])
+        back1_s[:, cols] = (dot(w2t[...], back2_s[:, cols]) * slope1_s[:, cols]).astype(BF)
+        add_blocks(5, dot_last(back1_s[:, cols], inputs_s[:, cols]), chunk == 0)
+
+    def input_part(chunk):
+        cols = slice(chunk * CHUNK, (chunk + 1) * CHUNK)
+        input_cot = dot(w1t[...], back1_s[:, cols])
         normed = normed_s[:, cols]
         state_part = inv_s[:, cols] * (
             input_cot - normed * jnp.mean(input_cot * normed, axis=0, keepdims=True))
@@ -307,7 +309,6 @@
         return sum(dot(jnp.concatenate([high_s[row], high_s[row + 1]], axis=1),
                        pack_m[row * LON:(row + 2) * LON, :]) for row in range(0, ROWS, 2)).astype(BF)
 
-    loads[7].wait()
     for chunk in range(CHUNKS // 2):
         backward(chunk)
     for red in early:
@@ -315,6 +316,10 @@
     for chunk in range(CHUNKS // 2, CHUNKS):
         backward(chunk)
     reds[-1].step0()
+    loads[7].wait()
+    for chunk in range(CHUNKS):
+        input_part(chunk)
+    reds[-1].step1()
 
     def send_halo(slot):
         row_send[slot, 0] = high_s[ROWS - 1]
@@ -337,7 +342,6 @@
                              for i, pair in enumerate(faces_pairs)).astype(BF)
     rim_copy(SUBSTEPS, 0).start()
     send_halo(0)
-    reds[-1].step1()
 
     def sides():
         sides_s[...] = dot(jnp.concatenate(
@@ -396,9 +400,18 @@
         out_nat[pl.ds(row, LEV, stride=ROWS), :] = new
 
     stores = [pltpu.make_async_copy(src, dst, store_sem.at[i]) for i, (src, dst) in enumerate(
-        ((out_nat, out_hbm), (first, first_hbm), (second, second_hbm), (third, third_hbm)))]
+        ((out_nat, out_hbm), (first, first_hbm), (third, third_hbm)))]
 
     third_red, second_red, first_red = reds
+    def put_second(other):
+        base = pl.multiple_of(64 * (1 - core if other else core), 64)
+        for i in range(4):
+            rows = pl.ds(pl.multiple_of(128 * i + base, 64), 64)
+            second[rows, :] = second_red.full[i, pl.ds(base, 64), :].astype(F32) * scale
+            store = pltpu.make_async_copy(second.at[rows], second_hbm.at[rows], second_sem.at[other, i])
+            store.start()
+            stores.append(store)
+
     inner(cot_a, cot_b)
     third_red.step2()
     second_red.step2()
@@ -419,6 +432,7 @@
     stores[0].start()
     first_red.step4()
     second_red.step4()
+    put_second(0)
     third_red.finish()
 
     def total(index):
@@ -429,16 +443,14 @@
     sum_third = total(4)
     for m in blocks:
         third[:, m] = sum_third[:, m].T
-    stores[3].start()
+    stores[2].start()
     first_red.finish()
     sum_first = total(5)
     for m in blocks:
         first[m, :] = sum_first[:, m]
     stores[1].start()
     second_red.finish()
-    for i, m in enumerate(blocks):
-        second[m, :] = total(i)
-    stores[2].start()
+    put_second(1)
     for store in stores:
         store.wait()
 
@@ -490,13 +502,13 @@
         *f32s(flat, flat), *bfs(flat, flat), *f32s(flat), *bfs(flat, flat),
         *bfs((HID, LEV), (HID, HID), (LEV, HID), (LEV, HID), (HID, HID), (HID, LEV)),
         *f32s((LEV, COLS), (1, COLS)), *bfs((LEV, COLS), (HID, COLS)), *f32s((HID, COLS)),
-        *bfs((HID, COLS), (2, HID, CHUNK)), *f32s((6, 128, 512)),
+        *bfs((HID, COLS), (2, HID, CHUNK), (HID, COLS)), *f32s((6, 128, 512)),
         *f32s((ROWS + 2,) + tile, (ROWS + 2,) + tile), *bfs(grid, grid), *f32s((COLS, 2 * LON)),
         *f32s(grid, grid, grid, (ROWS + 1,) + tile, grid),
         *bfs((2 * LON, 2 * LON), (2 * LON, COLS), (COLS, LON)),
         *f32s(flat, (HID, LEV), (HID, HID), (LEV, HID)),
         *bfs((SUBSTEPS + 1,) + tile, halo + tile, halo + tile, halo + tile),
-        dma((8,)), dma((4,)), dma(halo), dma(halo), dma(halo), dma(halo),
+        dma((8,)), dma((3,)), dma((2, 4)), dma(halo), dma(halo), dma(halo), dma(halo),
     ]
     for _, count, plane_first in ROUNDS:
         scratch += reduction_scratch(count, plane_first)

time: 43 us -> 44.6 us (1.037)
  Pallas kernels: 42.1 us -> 43.7 us
    pallas_call x1, Pallas kernels: 39.4 us -> 41 us  [local(): pl.pallas_call(functools.partial(kernel, scale, ROUNDS), out_shape=result...]
where the time goes in v4:
time: 44.6 us; the launch traced here: 44.5 us
  Pallas kernels  43.7 us (98%)
  between operations  0.8 us (2%)
    pallas_call x1, Pallas kernels, local(): pl.pallas_call(functools.partial(kernel, scale, ROUNDS), out_shape=result...  41 us
    pallas_call x1, Pallas kernels, local(): pl.pallas_call(finish_kernel, out_shape=results, in_specs=[hbm] * 4, out_...  2.71 us

profile of v4, /device:TPU:1, one launch (start us, length us, event | category | flops | bytes accessed | tf_op | source)
XLA Modules:
  0.0 44.5 jit_solution(2606205486102713005)
XLA Ops:
  0.6 41.0 %shard_map.111 = (f32[2048,128]{1,0:T(8,128)}, f32[512,128]{1,0:T(8,128)}, f32[512,512]{1,0:T(8,128)}, f32[128,512]{1,0:T(8,128)}) custom-call(bf16[2048,128]{1,0:T(8,128)(2,1)} %bitcast.7, bf16[2048,128]{1,0:T(8,128)(2,1)} %bitcast.8, f32[2048,128]{1,0:T(8,128)} %bitcast.6, bf16[2048,128]{1,0:T(8,128)(2,1)} %bitcast.9, bf16[2048,128]{1,0:T(8,128)(2,1)} %bitcast.10, ...), custom_call_target="tpu_custom_call" | custom-call | tf_op jit(solution)/shard_map/pallas_call | solution.py:517
  41.6 2.7 %shard_map.112 = (f32[2048,128]{1,0:T(8,128)}, f32[512,128]{1,0:T(8,128)}, f32[512,512]{1,0:T(8,128)}, f32[128,512]{1,0:T(8,128)}) custom-call(f32[2048,128]{1,0:T(8,128)} %get-tuple-element.12.refs_0_, f32[512,128]{1,0:T(8,128)} %get-tuple-element.13.refs_1_, f32[512,512]{1,0:T(8,128)} %get-tuple-element.14.refs_2_, f32[128,512]{1,0:T(8,128)} %get-tuple-element.15.refs_3_), custom_call_target="tpu_custom_call" | custom-call | tf_op jit(solution)/shard_map/pallas_call | solution.py:527

commit v5 on v3

--- a/solution.py
+++ b/solution.py
@@ -307,23 +307,6 @@
         return sum(dot(jnp.concatenate([high_s[row], high_s[row + 1]], axis=1),
                        pack_m[row * LON:(row + 2) * LON, :]) for row in range(0, ROWS, 2)).astype(BF)
 
-    loads[7].wait()
-    for chunk in range(CHUNKS // 2):
-        backward(chunk)
-    for red in early:
-        red.step1()
-    for chunk in range(CHUNKS // 2, CHUNKS):
-        backward(chunk)
-    reds[-1].step0()
-
-    def send_halo(slot):
-        row_send[slot, 0] = high_s[ROWS - 1]
-        row_send[slot, 1] = high_s[0]
-        send_rows(slot, (0, 1))
-        rim_send[slot] = packed()
-        rim_copy(slot, 0).start()
-        rim_copy(slot, 1).start()
-
     loads[5].wait()
     loads[6].wait()
     nat_a[...] = clon[...].astype(F32)
@@ -336,8 +319,23 @@
     rim_send[SUBSTEPS] = sum(dot(pair, pack_m[2 * i * LON:2 * (i + 1) * LON, :])
                              for i, pair in enumerate(faces_pairs)).astype(BF)
     rim_copy(SUBSTEPS, 0).start()
+    loads[7].wait()
+    backward(0)
+    for red in early:
+        red.step1()
+    for chunk in range(1, CHUNKS):
+        backward(chunk)
+    reds[-1].step0()
+
+    def send_halo(slot):
+        row_send[slot, 0] = high_s[ROWS - 1]
+        row_send[slot, 1] = high_s[0]
+        send_rows(slot, (0, 1))
+        rim_send[slot] = packed()
+        rim_copy(slot, 0).start()
+        rim_copy(slot, 1).start()
+
     send_halo(0)
-    reds[-1].step1()
 
     def sides():
         sides_s[...] = dot(jnp.concatenate(
@@ -351,6 +349,7 @@
         south_f[row + 1] = jnp.minimum(ahead, 0.0)
 
     loop(0, ROWS, split_lat)
+    reds[-1].step1()
     rim_copy(SUBSTEPS, 0).wait()
     wait_rows(SUBSTEPS, (0,))
     south_f[0] = jnp.minimum(row_recv[SUBSTEPS, 0].astype(F32), 0.0)

time: 43 us -> 42.7 us (level)
  no operation moved by 1% of the time
where the time goes in v5:
time: 42.7 us; the launch traced here: 42.6 us
  Pallas kernels  41.8 us (98%)
  between operations  0.8 us (2%)
    pallas_call x1, Pallas kernels, local(): pl.pallas_call(functools.partial(kernel, scale, ROUNDS), out_shape=result...  39.1 us
    pallas_call x1, Pallas kernels, local(): pl.pallas_call(finish_kernel, out_shape=results, in_specs=[hbm] * 4, out_...  2.71 us

profile of v5, /device:TPU:1, one launch (start us, length us, event | category | flops | bytes accessed | tf_op | source)
XLA Modules:
  0.0 42.6 jit_solution(18303041959801110115)
XLA Ops:
  0.6 39.1 %shard_map.111 = (f32[2048,128]{1,0:T(8,128)}, f32[512,128]{1,0:T(8,128)}, f32[512,512]{1,0:T(8,128)}, f32[128,512]{1,0:T(8,128)}) custom-call(bf16[2048,128]{1,0:T(8,128)(2,1)} %bitcast.7, bf16[2048,128]{1,0:T(8,128)(2,1)} %bitcast.8, f32[2048,128]{1,0:T(8,128)} %bitcast.6, bf16[2048,128]{1,0:T(8,128)(2,1)} %bitcast.9, bf16[2048,128]{1,0:T(8,128)(2,1)} %bitcast.10, ...), custom_call_target="tpu_custom_call" | custom-call | tf_op jit(solution)/shard_map/pallas_call | solution.py:504
  39.7 2.7 %shard_map.112 = (f32[2048,128]{1,0:T(8,128)}, f32[512,128]{1,0:T(8,128)}, f32[512,512]{1,0:T(8,128)}, f32[128,512]{1,0:T(8,128)}) custom-call(f32[2048,128]{1,0:T(8,128)} %get-tuple-element.12.refs_0_, f32[512,128]{1,0:T(8,128)} %get-tuple-element.13.refs_1_, f32[512,512]{1,0:T(8,128)} %get-tuple-element.14.refs_2_, f32[128,512]{1,0:T(8,128)} %get-tuple-element.15.refs_3_), custom_call_target="tpu_custom_call" | custom-call | tf_op jit(solution)/shard_map/pallas_call | solution.py:514

commit v6 on v5

--- a/solution.py
+++ b/solution.py
@@ -23,7 +23,7 @@
 CHUNKS = ROWS // CHUNK_ROWS
 PLANE = 16
 DEPTH = 8
-ROUNDS = ((4, 1, False), (0, 4, True), (5, 1, False))
+ROUNDS = ((3, 2, False), (0, 3, True), (5, 1, False))
 FINISH_ROWS = 512
 
 

time: 42.7 us -> 41.7 us (0.977)
  Pallas kernels: 41.8 us -> 40.8 us
    pallas_call x1, Pallas kernels: 39.1 us -> 38 us  [local(): pl.pallas_call(functools.partial(kernel, scale, ROUNDS), out_shape=result...]
where the time goes in v6:
time: 41.7 us; the launch traced here: 41.6 us
  Pallas kernels  40.8 us (98%)
  between operations  0.8 us (2%)
    pallas_call x1, Pallas kernels, local(): pl.pallas_call(functools.partial(kernel, scale, ROUNDS), out_shape=result...  38 us
    pallas_call x1, Pallas kernels, local(): pl.pallas_call(finish_kernel, out_shape=results, in_specs=[hbm] * 4, out_...  2.71 us

profile of v6, /device:TPU:1, one launch (start us, length us, event | category | flops | bytes accessed | tf_op | source)
XLA Modules:
  0.0 41.6 jit_solution(13772911844581620727)
XLA Ops:
  0.6 38.0 %shard_map.111 = (f32[2048,128]{1,0:T(8,128)}, f32[512,128]{1,0:T(8,128)}, f32[512,512]{1,0:T(8,128)}, f32[128,512]{1,0:T(8,128)}) custom-call(bf16[2048,128]{1,0:T(8,128)(2,1)} %bitcast.7, bf16[2048,128]{1,0:T(8,128)(2,1)} %bitcast.8, f32[2048,128]{1,0:T(8,128)} %bitcast.6, bf16[2048,128]{1,0:T(8,128)(2,1)} %bitcast.9, bf16[2048,128]{1,0:T(8,128)(2,1)} %bitcast.10, ...), custom_call_target="tpu_custom_call" | custom-call | tf_op jit(solution)/shard_map/pallas_call | solution.py:504
  38.7 2.7 %shard_map.112 = (f32[2048,128]{1,0:T(8,128)}, f32[512,128]{1,0:T(8,128)}, f32[512,512]{1,0:T(8,128)}, f32[128,512]{1,0:T(8,128)}) custom-call(f32[2048,128]{1,0:T(8,128)} %get-tuple-element.12.refs_0_, f32[512,128]{1,0:T(8,128)} %get-tuple-element.13.refs_1_, f32[512,512]{1,0:T(8,128)} %get-tuple-element.14.refs_2_, f32[128,512]{1,0:T(8,128)} %get-tuple-element.15.refs_3_), custom_call_target="tpu_custom_call" | custom-call | tf_op jit(solution)/shard_map/pallas_call | solution.py:514
